TPU v7x, 128 devices: a whole 4x4x4 slice. The times are simulated.
128 devices in a mesh: ctx: 16 (over x, z_lo, core), vocab: 8 (over y, z_hi).
Axes of the slice: x: 4, y: 4, z: 4 (z_hi: 2, z_lo: 2; z = z_hi * 2 + z_lo), core: 2. Of those that a mesh axis runs over, the one named last changes fastest.
Arguments:
- hidden: bfloat16 [2048, 6144], P('ctx'), may hold values from -16 to 16
- labels: int32 [2048], P('ctx'), may hold values from 0 to 65535
- head_weight: bfloat16 [6144, 65536], P(None, ('ctx', 'vocab')), may hold values from -0.31894398 to 0.31894398
Outputs:
- token_loss: float32 [2048], P('ctx')
- head_grad: float32 [6144, 65536], P(None, ('ctx', 'vocab'))
All inputs are finite; a program needn't handle non-finite values.
Results may differ from a plain program's by a relative error of at most 0.0021.
Values may be sent and summed in bfloat16 or wider, within the bound.
A program may use at most 128 MiB of HBM per device.

v0:
```python
import jax
import jax.numpy as jnp
from jax import lax
from jax.sharding import PartitionSpec as P

z_weight = 0.0001


def on_device(hidden, labels, head_weight):
    tok_rows = hidden.shape[0]
    columns_here = head_weight.shape[1]
    first_column = (
        lax.axis_index("ctx") * lax.axis_size("vocab") + lax.axis_index("vocab")
    ) * columns_here
    targets = lax.all_gather(labels, "ctx", axis=0, tiled=True)
    row_count = targets.shape[0]
    all_rows = lax.all_gather(hidden, "ctx", axis=0, tiled=True)
    logits = jnp.dot(all_rows, head_weight, preferred_element_type=jnp.float32)
    columns = lax.broadcasted_iota(jnp.int32, (row_count, columns_here), 1)
    label_mask = columns == (targets - first_column)[:, None]
    label_part = jnp.sum(jnp.where(label_mask, logits, 0.0), axis=1)
    local_max = jnp.max(logits, axis=1)
    row_top = lax.pmax(local_max, ("ctx", "vocab"))
    local_sum = jnp.sum(jnp.exp(logits - row_top[:, None]), axis=1)
    row_total, label_logit = lax.psum((local_sum, label_part), ("ctx", "vocab"))
    log_partition = row_top + jnp.log(row_total)
    token_loss = log_partition - label_logit + z_weight * log_partition * log_partition
    softmax_rows = jnp.exp(logits - log_partition[:, None])
    logit_slope = (
        (1.0 + 2.0 * z_weight * log_partition)[:, None] * softmax_rows
        - label_mask.astype(jnp.float32)
    ).astype(jnp.bfloat16)
    head_grad = lax.dot_general(
        all_rows, logit_slope, (((0,), (0,)), ((), ())), preferred_element_type=jnp.float32
    )
    own_loss = lax.dynamic_slice_in_dim(token_loss, lax.axis_index("ctx") * tok_rows, tok_rows)
    return (own_loss, head_grad)


def solution(mesh):
    return jax.shard_map(
        on_device,
        mesh=mesh,
        in_specs=(P("ctx", None), P("ctx"), P(None, ("ctx", "vocab"))),
        out_specs=(P("ctx"), P(None, ("ctx", "vocab"))),
        check_vma=False,
    )
```

profile of v0, /device:TPU:1, one launch (start us, length us, event | category | flops | bytes accessed | tf_op | source)
XLA Modules:
  0.0 338.7 jit_solution(7826303181338605410)
XLA Ops:
  7.2 0.0 all-gather.3.cloned.1.call-start
  7.2 0.7 all-gather.3.cloned.1.call-update
  7.9 21.4 %all-gather = s32[16,1,128]{2,1,0:T(1,128)S(1)} all-gather(s32[1,1,128]{2,1,0:T(1,128)} %bitcast.12), channel_id=1, replica_groups=mesh['ctx'=16,'vocab'=8] {'ctx'}, dimensions={0}, use_global_device_ids=true | all-gather | bytes 8704 | tf_op jit(solution)/shard_map/all_gather | solution.py:15
  29.3 115.3 %all-gather.3.cloned.1.call-done = bf16[2048,6144]{1,0:T(8,128)(2,1)} async-done(((bf16[128,6144]{1,0:T(8,128)(2,1)}), bf16[2048,6144]{1,0:T(8,128)(2,1)}) %all-gather.3.cloned.1.call-update) | async-done | bytes 25165840 | tf_op jit(solution)/shard_map/all_gather | solution.py:17
  144.6 20.0 %fusion.4 = (f32[2048]{0:T(1024)S(1)}, f32[2048,512]{0,1:T(8,128)}) fusion(bf16[2048,6144]{1,0:T(8,128)(2,1)} %all-gather.3.cloned.1.call-done, bf16[6144,512]{1,0:T(8,128)(2,1)} %param.5), kind=kOutput, calls=%fused_computation.14 | convolution fusion | flops 12885948416 | bytes 35659776 | tf_op jit(solution)/shard_map/dot_general | solution.py:18
  164.5 65.6 %pmax.7 = f32[2048]{0:T(1024)S(1)} all-reduce(f32[2048]{0:T(1024)S(1)} %get-tuple-element.12), channel_id=1, replica_groups=mesh['ctx'=16,'vocab'=8] {'ctx','vocab'}, use_global_device_ids=true, to_apply=%region_1.2 | all-reduce | flops 2048 | bytes 16384 | tf_op jit(solution)/shard_map/pmax | solution.py:23
  230.2 3.3 exponential_reduce_fusion
  233.5 63.2 %all-reduce = (f32[2048]{0:T(1024)S(1)}, f32[2048]{0:T(1024)S(1)}) all-reduce(f32[2048]{0:T(1024)S(1)} %get-tuple-element.7, f32[2048]{0:T(1024)S(1)} %get-tuple-element.6), channel_id=1, replica_groups=mesh['ctx'=16,'vocab'=8] {'ctx','vocab'}, use_global_device_ids=true, to_apply=%region_5.6 | all-reduce | flops 4096 | bytes 32768 | tf_op jit(solution)/shard_map/psum | solution.py:25
  296.7 22.0 %convolution_bitcast_fusion = f32[6144,512]{0,1:T(8,128)} fusion(bf16[2048,6144]{1,0:T(8,128)(2,1)} %all-gather.3.cloned.1.call-done, f32[2048,512]{0,1:T(8,128)} %get-tuple-element.13, f32[2048]{0:T(1024)S(1)} %get-tuple-element.11, f32[2048]{0:T(1024)S(1)} %get-tuple-element.10, s32[2048]{0:T(1024)S(1)} %bitcast.10), kind=kOutput, calls=%fused_computation | convolution fusion | flops 12891193344 | bytes 41967616 | tf_op jit(solution)/shard_map/dot_general | solution.py:33
  318.7 12.6 %copy.6 = f32[6144,512]{1,0:T(8,128)} copy(f32[6144,512]{0,1:T(8,128)} %convolution_bitcast_fusion) | data formatting | bytes 25165824
  331.3 0.6 fusion.3
  (2 shorter events, 0.0 us)
Async XLA Ops:
  7.2 137.4 %all-gather.3.cloned.1.call-start = ((), (), s32[]{:S(2)}) async-start(), calls=%async_computation | async-start | bytes 26738688 | tf_op jit(solution)/shard_map/all_gather | solution.py:17
Sparse Core Ops, SparseCore 0:
  9.7 134.8 all-gather.2
where the time goes:
time: 339 us
  blocking collectives  150 us (44%)
  waiting for transfers between devices  116 us (34%)
  matrix products  42 us (12%)
  between operations  14 us (4%)
  local copies, waits for them, and re-layouts  12.6 us (4%)
  other arithmetic  3.88 us (1%)
    all_gather x1, waiting for transfers between devices, on_device(): all_rows = lax.all_gather(hidden, 'ctx', axis=0, tiled=True)  115 us
    pmax x1, blocking collectives, on_device(): row_top = lax.pmax(local_max, ('ctx', 'vocab'))  65.6 us
    psum x1, blocking collectives, on_device(): row_total, label_logit = lax.psum((local_sum, label_part), ('ctx', 'vocab'))  63.2 us
    dot_general x1, matrix products, on_device(): lax.dot_general(all_rows, logit_slope, (((0,), (0,)), ((), ())), preferre...  22 us
    all_gather x1, blocking collectives, on_device(): targets = lax.all_gather(labels, 'ctx', axis=0, tiled=True)  21.4 us
    dot_general x1, matrix products, on_device(): logits = jnp.dot(all_rows, head_weight, preferred_element_type=jnp.float32)  20 us
    unnamed x1, local copies, waits for them, and re-layouts  12.6 us
  transfers between devices with their start and end apart: 1, of which 1 were waited for; matrix products, arithmetic and copies ran while one was open for 0% of the time, Pallas kernels for 0%

commit v1 on v0

v1 whole, which is shorter than its diff:
```python
import heapq
import jax
import jax.numpy as jnp
from jax import lax
from jax.experimental import pallas as pl
from jax.experimental.pallas import tpu as pltpu
from jax.sharding import PartitionSpec as P

MESH = pl.DeviceIdType.MESH
z_weight = 0.0001

REGIONS = ("F", "F'", "C", "S'", "S")
BLOCKS = ("0", "L", "R", "2")
LINKS = ("x+", "x-", "z+", "z-", "y+", "y-")
ORDER = {"x": ("F", "F'", "C", "S'"), "z": ("F", "F'", "C"), "y": ("F", "F'")}


def region_rows(half):
    unit = half // 48
    edge, wide = 9 * unit, 10 * unit
    return dict(zip(REGIONS, (edge, wide, wide, wide, edge)))


def starts_of(rows):
    starts, at = {}, 0
    for name in REGIONS:
        starts[name] = at
        at += rows[name]
    return starts


def onward(key):
    _, block, region, part = key
    links = []
    if block[0] != "Z":
        if region != "S":
            if block == "0":
                links += ["x+", "x-"]
            if (block, part) == ("L", 0):
                links.append("x+")
            if (block, part) == ("R", 1):
                links.append("x-")
        if region in ORDER["z"]:
            links.append(("z+", "z-")[part])
        if region == "F" and block != "0":
            links.append(("y+", "y-")[part])
    elif region in ORDER["y"]:
        links.append(("y+", "y-")[part])
    return links


def landing(link, key):
    phase, block, region, part = key
    if link[0] == "x":
        block = "2" if block != "0" else ("L" if link == "x+" else "R")
    elif link[0] == "z":
        block = "Z" + block
    else:
        region = {"F": "S", "F'": "S'"}[region]
    return phase, block, region, part


def plan(halves, tasks, first):
    row_link, row_pair, hop, pair_hop, issue, ahead = 256 / 45.5e3, 256 / 500e3, 1.7, 1.0, 0.04, 3.0
    rows = [region_rows(half) for half in halves]
    now, tick = first, 0
    busy = dict.fromkeys(LINKS + ("pair",), 0.0)
    queue = {link: [] for link in LINKS}
    coming, have, steps = [], set(), []
    tasks = list(tasks)
    near = {"0": 0, "L": 1, "R": 1, "2": 2}

    def post(when, what):
        nonlocal tick
        tick += 1
        heapq.heappush(coming, (when, tick, what))

    def rank(link, key):
        return key[0], ORDER[link[0]].index(key[2]), near[key[1][-1]], key[3]

    def pump():
        nonlocal now
        for link in LINKS:
            while queue[link] and busy[link] - now < ahead:
                key = min(queue[link], key=lambda k: rank(link, k))
                queue[link].remove(key)
                steps.append(("send", link, key))
                now += issue
                busy[link] = max(busy[link], now) + rows[key[0]][key[2]] // 2 * row_link
                post(busy[link] + hop, ("piece", landing(link, key)))

    for phase in range(len(halves)):
        for region in ORDER["x"]:
            for part in (0, 1):
                key = (phase, "0", region, part)
                for link in onward(key):
                    queue[link].append(key)
    while True:
        while coming and coming[0][0] <= now:
            kind, key = heapq.heappop(coming)[2]
            if kind == "piece":
                have.add(("here", key))
                steps.append(("take", key))
                for link in onward(key):
                    queue[link].append(key)
                busy["pair"] = max(busy["pair"], now) + rows[key[0]][key[2]] // 2 * row_pair
                post(busy["pair"] + pair_hop, ("there", key))
                now += 2 * issue
            else:
                have.add((kind, key))
            pump()
        pump()
        ready = [task for task in tasks if all(need in have for need in task[2])]
        if ready:
            name, took, _, reply = ready[0]
            tasks.remove(ready[0])
            steps.append(("task", name))
            now += took
            have.add(("done", name))
            if reply:
                post(now + reply, ("reply", name))
        elif coming:
            now = max(now, coming[0][0])
        else:
            break
    assert not tasks and not any(queue.values())
    return steps, now


def head(hidden, labels, head_weight):
    tok, depth = hidden.shape
    cols = head_weight.shape[1]
    half = depth // 2
    rows = region_rows(half)
    starts = starts_of(rows)
    n_ctx, n_vocab, phases, n_x = 16, 8, 2, 4
    per_phase = n_ctx // phases
    kpiece = 1024
    n_k = half // kpiece
    w_step = 512
    n_w = depth // w_step
    w_slots = 3
    grad_step = 1024
    n_grad = depth // grad_step

    keys = []
    for phase in range(phases):
        for block in BLOCKS[1:] + tuple("Z" + b for b in BLOCKS):
            for region in REGIONS:
                keys += [(phase, block, region, part) for part in (0, 1)]
    sem_of = {key: i for i, key in enumerate(keys)}
    groups = [(phase, b, region) for phase in range(phases) for b in BLOCKS for region in REGIONS]
    group_of = {g: i for i, g in enumerate(groups)}

    tasks = [(("w", i), 0.3, (), 0) for i in range(n_w)]
    for phase in range(phases):
        tasks.append((("merge1", phase), 0.3, (("reply", ("stats", phase)),), 4.0))
        tasks.append((("merge2", phase), 0.3, (("reply", ("merge1", phase)),), 0))
        for b in BLOCKS:
            tasks.append((("slope", phase, b), 0.3, (("done", ("merge2", phase)),), 0))
    for phase in range(phases):
        for k in range(n_k):
            for b in BLOCKS:
                needs = [("done", ("w", n_w - 1))]
                for region in REGIONS:
                    if starts[region] < (k + 1) * kpiece and starts[region] + rows[region] > k * kpiece:
                        for part in (0, 1):
                            for block in ((b, "Z" + b) if b != "0" else ("Z0",)):
                                key = (phase, block, region, part)
                                needs += [("here", key), ("there", key)]
                tasks.append((("logits", phase, k, b), 0.65, tuple(needs), 0))
        tasks.append((
            ("stats", phase), 1.0,
            tuple(("done", ("logits", phase, k, b)) for k in range(n_k) for b in BLOCKS), 5.0,
        ))
    for phase in range(phases):
        for i in range(n_grad):
            tasks.append((
                ("grad", phase, i), 1.5, tuple(("done", ("slope", phase, b)) for b in BLOCKS), 0,
            ))
    steps, _ = plan([half] * phases, tasks, 0.0)

    def kernel(hid_hbm, lab_ref, w_hbm, grad, loss, hid, H, wst, WT, LT, ST, LB, S1, S2, LP,
               hid_sem, w_sem, recv, pair_recv, own_recv, own_recv2, send, own_send, st_send, st_recv, lb_send, lb_recv):
        ctx, voc = lax.axis_index("ctx"), lax.axis_index("vocab")
        core, zl, x = ctx % 2, (ctx // 2) % 2, ctx // 4
        zh, y = voc % 2, voc // 2
        q = y % 2

        def at(xx, zz, cc):
            return (xx * 2 + zz) * 2 + cc

        own_hid = pltpu.make_async_copy(hid_hbm, hid, hid_sem)
        own_hid.start()

        def w_copy(i):
            return pltpu.make_async_copy(
                w_hbm.at[pl.ds(i * w_step, w_step), :], wst.at[i % w_slots], w_sem.at[i % w_slots])

        for i in range(w_slots):
            w_copy(i).start()

        right, left, across = (x + 1) % 4, (x + 3) % 4, (x + 2) % 4
        up, down = voc + 2, voc + 6
        zp, zm = (zh * 2 + zl + 1) % 4, (zh * 2 + zl + 3) % 4
        device = {
            "x+": (at(right, zl, core), voc),
            "x-": (at(left, zl, core), voc),
            "z+": (at(x, zp % 2, core), y * 2 + zp // 2),
            "z-": (at(x, zm % 2, core), y * 2 + zm // 2),
            "y+": (ctx, up % 8),
            "y-": (ctx, down % 8),
            "pair": (at(x, zl, 1 - core), voc),
        }
        ctx_peers = [((ctx + i) % n_ctx, voc) for i in range(1, n_ctx)]
        voc_peers = [(ctx, (voc + i) % n_vocab) for i in range(1, n_vocab)]
        cross = (at(x, 1 - zl, core), y * 2 + 1 - zh)

        barrier = pltpu.get_barrier_semaphore()
        for peer in ctx_peers + voc_peers + [cross]:
            pl.semaphore_signal(barrier, inc=1, device_id=peer, device_id_type=MESH)

        xs = {"0": x, "L": left, "R": right, "2": across}
        mine = x * 2 + zl

        def slot(phase, block):
            if block[0] == "Z":
                return phase * per_phase + xs[block[1]] * 2 + 1 - zl
            return phase * per_phase + xs[block] * 2 + zl

        def region_at(region, which):
            ahead = starts[region]
            back = half - starts[region] - rows[region]
            return which * half + jnp.where(q == 0, ahead, back)

        begin = {region: region_at(region, core) for region in REGIONS}
        begin_pair = {region: region_at(region, 1 - core) for region in REGIONS}

        def piece(key):
            phase, block, region, part = key
            n = rows[region] // 2
            return H.at[slot(phase, block), pl.ds(pl.multiple_of(begin[region] + part * n, 16), n), :]

        def link_copy(link, key):
            ref = piece(key)
            i = LINKS.index(link)
            return pltpu.make_async_remote_copy(
                src_ref=ref, dst_ref=ref, send_sem=send.at[key[0], i], recv_sem=recv.at[sem_of[landing(link, key)]],
                device_id=device[link], device_id_type=MESH)

        def take(key):
            ref = piece(key)
            pltpu.make_async_remote_copy(
                src_ref=ref, dst_ref=ref, send_sem=send.at[0, 0], recv_sem=recv.at[sem_of[key]],
                device_id=device["pair"], device_id_type=MESH).wait_recv()
            phase, block, region, _ = key
            pltpu.make_async_remote_copy(
                src_ref=ref, dst_ref=ref, send_sem=send.at[phase, 6],
                recv_sem=pair_recv.at[group_of[(phase, block[-1], region)]],
                device_id=device["pair"], device_id_type=MESH).start()

        def drain(n_rows, sem):
            full, rest = divmod(n_rows, depth)
            assert full == 0 or rest == 0
            ref = H.at[0, pl.ds(0, n_rows), :] if full == 0 else H.at[pl.ds(0, full)]
            return pltpu.make_async_remote_copy(
                src_ref=ref, dst_ref=ref, send_sem=sem, recv_sem=sem, device_id=device["pair"], device_id_type=MESH)

        own_hid.wait()
        own_slot = core * per_phase + mine
        for i in range(depth // 1024):
            H[own_slot, pl.ds(i * 1024, 1024), :] = hid[:, pl.ds(i * 1024, 1024)].T
        LB[ctx] = lab_ref[...]
        pl.semaphore_wait(barrier, len(ctx_peers) + len(voc_peers) + 1)

        def own_copy(region, theirs):
            first = (begin_pair if theirs else begin)[region]
            ref = H.at[own_slot, pl.ds(pl.multiple_of(first, 16), rows[region]), :]
            sem = own_recv.at[REGIONS.index(region)] if theirs else own_recv2
            return pltpu.make_async_remote_copy(
                src_ref=ref, dst_ref=ref, send_sem=own_send, recv_sem=sem,
                device_id=device["pair"], device_id_type=MESH)

        for region in REGIONS:
            own_copy(region, True).start()

        def own_wait(region, phase):
            @pl.when(core != phase)
            def _():
                ref = H.at[phase * per_phase + mine, pl.ds(pl.multiple_of(begin[region], 16), rows[region]), :]
                pltpu.make_async_remote_copy(
                    src_ref=ref, dst_ref=ref, send_sem=own_send, recv_sem=own_recv.at[REGIONS.index(region)],
                    device_id=device["pair"], device_id_type=MESH).wait_recv()

        own_seen, rest_sent, rest_seen, groups_seen = set(), [False], set(), set()

        def send_rest():
            for region in REGIONS:
                own_copy(region, False).start()
            for peer in ctx_peers:
                pltpu.make_async_remote_copy(
                    src_ref=LB.at[ctx], dst_ref=LB.at[ctx], send_sem=lb_send, recv_sem=lb_recv,
                    device_id=peer, device_id_type=MESH).start()

        def need_own(region, phase):
            if (region, phase) not in own_seen:
                own_seen.add((region, phase))
                own_wait(region, phase)

        def need_rest(phase):
            if phase not in rest_seen:
                rest_seen.add(phase)

                @pl.when(core != phase)
                def _():
                    drain(half, own_recv2).wait_recv()

        def need_group(phase, b, region):
            if (phase, b, region) not in groups_seen:
                groups_seen.add((phase, b, region))
                drain(rows[region] * (1 if b == "0" else 2), pair_recv.at[group_of[(phase, b, region)]]).wait_recv()

        def w_task(i):
            w_copy(i).wait()
            WT[:, pl.ds(i * w_step, w_step)] = wst[i % w_slots].T
            if i + w_slots < n_w:
                w_copy(i + w_slots).start()

        def logits_task(phase, k, b):
            for region in REGIONS:
                if starts[region] < (k + 1) * kpiece and starts[region] + rows[region] > k * kpiece:
                    need_group(phase, b, region)
                    if b == "0":
                        need_own(region, phase)
            if b == "0":
                need_rest(phase)
            xb = xs[b]
            s0 = phase * per_phase + xb * 2
            total = None
            for which in (core, 1 - core):
                off = which * half + jnp.where(q == 0, k * kpiece, half - (k + 1) * kpiece)
                off = pl.multiple_of(off, 1024)
                ks = pl.ds(off, kpiece)
                block = jnp.concatenate([H[s0, ks, :], H[s0 + 1, ks, :]], axis=1)
                part = jnp.dot(WT[:, ks], block, preferred_element_type=jnp.float32)
                total = part if total is None else total + part
            if k == 0:
                LT[phase, xb] = total
            else:
                LT[phase, xb] += total

        first_col = (ctx * n_vocab + voc) * cols
        label_seen = [False]

        def label_mask(phase, xb):
            lab = jnp.concatenate([LB[at(xb, 0, phase)], LB[at(xb, 1, phase)]], axis=1)
            ids = lax.broadcasted_iota(jnp.int32, (cols, 2 * tok), 0)
            return ids == lab - first_col

        def stats_task(phase):
            if not label_seen[0]:
                label_seen[0] = True
                pltpu.make_async_remote_copy(
                    src_ref=LB.at[pl.ds(0, n_ctx - 1)], dst_ref=LB.at[pl.ds(0, n_ctx - 1)], send_sem=lb_send,
                    recv_sem=lb_recv, device_id=device["pair"], device_id_type=MESH).wait_recv()
            for xb in range(n_x):
                lt = LT[phase, xb]
                top = jnp.max(lt, axis=0, keepdims=True)
                total = jnp.sum(jnp.exp(lt - top), axis=0, keepdims=True)
                label = jnp.sum(jnp.where(label_mask(phase, xb), lt, 0.0), axis=0, keepdims=True)
                for i, row in enumerate((top, total, label)):
                    S1[phase, ctx, i, 2 * xb:2 * xb + 1, :] = row[:, :tok]
                    S1[phase, ctx, i, 2 * xb + 1:2 * xb + 2, :] = row[:, tok:]
            for peer in ctx_peers:
                stat_copy(S1, phase, ctx, 0, peer).start()

        def stat_copy(buf, phase, index, stage, peer):
            ref = buf.at[phase, index]
            return pltpu.make_async_remote_copy(
                src_ref=ref, dst_ref=ref, send_sem=st_send.at[phase, stage], recv_sem=st_recv.at[phase, stage],
                device_id=peer, device_id_type=MESH)

        def stat_all(buf, phase, stage, n):
            ref = buf.at[phase, pl.ds(0, n - 1)]
            return pltpu.make_async_remote_copy(
                src_ref=ref, dst_ref=ref, send_sem=st_send.at[phase, stage], recv_sem=st_recv.at[phase, stage],
                device_id=device["pair"], device_id_type=MESH)

        def merged(buf, phase, n):
            tops = [buf[phase, i, 0] for i in range(n)]
            top = tops[0]
            for t in tops[1:]:
                top = jnp.maximum(top, t)
            total = sum(buf[phase, i, 1] * jnp.exp(tops[i] - top) for i in range(n))
            label = sum(buf[phase, i, 2] for i in range(n))
            return top, total, label

        def merge1_task(phase):
            stat_all(S1, phase, 0, n_ctx).wait_recv()
            for i, row in enumerate(merged(S1, phase, n_ctx)):
                S2[phase, voc, i] = row
            for peer in voc_peers:
                stat_copy(S2, phase, voc, 1, peer).start()

        def merge2_task(phase):
            stat_all(S2, phase, 1, n_vocab).wait_recv()
            top, total, label = merged(S2, phase, n_vocab)
            lp = top + jnp.log(total)
            LP[phase, 0] = lp
            LP[phase, 1] = lp - label + z_weight * lp * lp

            @pl.when(core == phase)
            def _():
                loss[...] = LP[phase, 1, pl.ds(mine, 1), :]

        def slope_task(phase, b):
            xb = BLOCKS.index(b)
            lp = jnp.concatenate([LP[phase, 0, 2 * xb:2 * xb + 1, :], LP[phase, 0, 2 * xb + 1:2 * xb + 2, :]], axis=1)
            soft = jnp.exp(LT[phase, xb] - lp)
            hot = jnp.where(label_mask(phase, xb), 1.0, 0.0)
            ST[phase, xb] = ((1.0 + 2.0 * z_weight * lp) * soft - hot).astype(jnp.bfloat16)

        def grad_task(phase, i):
            rs = pl.ds(i * grad_step, grad_step)
            lhs = jnp.concatenate([H[phase * per_phase + b, rs, :] for b in range(per_phase)], axis=1)
            rhs = jnp.concatenate([ST[phase, xb] for xb in range(n_x)], axis=1)
            part = lax.dot_general(lhs, rhs, (((1,), (1,)), ((), ())), preferred_element_type=jnp.float32)
            if phase == 0:
                grad[rs, :] = part
            else:
                grad[rs, :] += part

        run = {"w": w_task, "logits": logits_task, "stats": stats_task, "merge1": merge1_task,
               "merge2": merge2_task, "slope": slope_task, "grad": grad_task}
        for step in steps:
            if step[0] == "send":
                _, link, key = step
                if key[1] == "0":
                    need_own(key[2], key[0])
                link_copy(link, key).start()
            elif step[0] == "take":
                take(step[1])
            else:
                if not rest_sent[0]:
                    rest_sent[0] = True
                    send_rest()
                name = step[1]
                run[name[0]](*name[1:])

        for phase in range(phases):
            for i, link in enumerate(LINKS):
                n = sum(rows[s[2][2]] // 2 for s in steps if s[0] == "send" and s[1] == link and s[2][0] == phase)
                drain(n, send.at[phase, i]).wait_send()
            ref = H.at[pl.ds(0, 7), pl.ds(0, half), :]
            pltpu.make_async_remote_copy(
                src_ref=ref, dst_ref=ref, send_sem=send.at[phase, 6], recv_sem=own_recv2,
                device_id=device["pair"], device_id_type=MESH).wait_send()
            stat_all(S1, phase, 0, n_ctx).wait_send()
            stat_all(S2, phase, 1, n_vocab).wait_send()
        drain(depth, own_send).wait_send()
        pltpu.make_async_remote_copy(
            src_ref=LB.at[pl.ds(0, n_ctx - 1)], dst_ref=LB.at[pl.ds(0, n_ctx - 1)], send_sem=lb_send,
            recv_sem=lb_recv, device_id=device["pair"], device_id_type=MESH).wait_send()

    bf16, f32 = jnp.bfloat16, jnp.float32
    dma = pltpu.SemaphoreType.DMA
    grad, loss = pl.pallas_call(
        kernel,
        name="head",
        out_shape=(pltpu.VMEM((depth, cols), f32), pltpu.VMEM((1, tok), f32)),
        in_specs=[pl.BlockSpec(memory_space=pl.ANY), pl.BlockSpec(memory_space=pltpu.VMEM),
                  pl.BlockSpec(memory_space=pl.ANY)],
        out_specs=(pl.BlockSpec(memory_space=pltpu.VMEM), pl.BlockSpec(memory_space=pltpu.VMEM)),
        scratch_shapes=[
            pltpu.VMEM((tok, depth), bf16),
            pltpu.VMEM((n_ctx, depth, tok), bf16),
            pltpu.VMEM((w_slots, w_step, cols), bf16),
            pltpu.VMEM((cols, depth), bf16),
            pltpu.VMEM((phases, n_x, cols, 2 * tok), f32),
            pltpu.VMEM((phases, n_x, cols, 2 * tok), bf16),
            pltpu.VMEM((n_ctx, 1, tok), jnp.int32),
            pltpu.VMEM((phases, n_ctx, 3, per_phase, tok), f32),
            pltpu.VMEM((phases, n_vocab, 3, per_phase, tok), f32),
            pltpu.VMEM((phases, 2, per_phase, tok), f32),
            dma, dma((w_slots,)), dma((len(keys),)), dma((len(groups),)), dma((len(REGIONS),)), dma,
            dma((phases, 7)), dma, dma((phases, 2)), dma((phases, 2)), dma, dma,
        ],
        compiler_params=pltpu.CompilerParams(
            collective_id=0, has_side_effects=True, vmem_limit_bytes=48 * 2**20),
    )(hidden, labels.reshape(1, tok), head_weight)
    return loss.reshape(tok), grad


def solution(mesh):
    return jax.shard_map(
        head,
        mesh=mesh,
        in_specs=(P("ctx", None), P("ctx"), P(None, ("ctx", "vocab"))),
        out_specs=(P("ctx"), P(None, ("ctx", "vocab"))),
        check_vma=False,
    )
```

time: 339 us -> 94.2 us (0.28)
  blocking collectives: 150 us -> 0 us
  waiting for transfers between devices: 116 us -> 0 us
  Pallas kernels: 0 us -> 88 us
  matrix products: 42 us -> 0 us
  between operations: 14 us -> 0.64 us
  local copies, waits for them, and re-layouts: 12.6 us -> 5.29 us
  other arithmetic: 3.88 us -> 0 us
    all_gather x1 -> x0, waiting for transfers between devices: 115 us -> none  [on_device(): all_rows = lax.all_gather(hidden, 'ctx', axis=0, tiled=True)]
    pallas_call x0 -> x1, Pallas kernels: none -> 88 us  [head(): pl.pallas_call(kernel, name='head', out_shape=(pltpu.VMEM((depth, cols),...]
    pmax x1 -> x0, blocking collectives: 65.6 us -> none  [on_device(): row_top = lax.pmax(local_max, ('ctx', 'vocab'))]
    psum x1 -> x0, blocking collectives: 63.2 us -> none  [on_device(): row_total, label_logit = lax.psum((local_sum, label_part), ('ctx', 'vocab'))]
    dot_general x2 -> x0, matrix products: 42 us -> none  [the longest x1 22 us: on_device(): lax.dot_general(all_rows, logit_slope, (((0,), (0,)), ((), ())), preferre...]
    all_gather x1 -> x0, blocking collectives: 21.4 us -> none  [on_device(): targets = lax.all_gather(labels, 'ctx', axis=0, tiled=True)]
    unnamed x1 -> x2, local copies, waits for them, and re-layouts: 12.6 us -> 5.29 us
  transfers between devices with their start and end apart: 1 -> 0, of which waited for: 1 -> 0; matrix products, arithmetic and copies ran while one was open for 0% -> 0% of each run, Pallas kernels for 0% -> 0%
where the time goes in v1:
time: 94.2 us; the launch traced here: 94 us
  Pallas kernels  88 us (93%)
  local copies, waits for them, and re-layouts  5.29 us (6%)
    pallas_call x1, Pallas kernels, head(): pl.pallas_call(kernel, name='head', out_shape=(pltpu.VMEM((depth, cols),...  88 us
    unnamed x2, local copies, waits for them, and re-layouts  5.29 us

profile of v1, /device:TPU:1, one launch (start us, length us, event | category | flops | bytes accessed | tf_op | source)
XLA Modules:
  0.0 94.0 jit_solution(2748445114705628746)
XLA Ops:
  0.6 88.0 %head.1 = (f32[6144,512]{1,0:T(8,128)S(1)}, f32[1,128]{1,0:T(1,128)S(1)}) custom-call(bf16[128,6144]{1,0:T(8,128)(2,1)} %hid_hbm.1, s32[1,128]{1,0:T(1,128)} %bitcast.3, bf16[6144,512]{1,0:T(8,128)(2,1)} %w_hbm.1), custom_call_target="tpu_custom_call" | custom-call | tf_op jit(solution)/shard_map/head/pallas_call | solution.py:467
  88.7 0.5 copy.7
  89.2 4.8 %copy.8 = f32[6144,512]{1,0:T(8,128)} copy(f32[6144,512]{1,0:T(8,128)S(1)} %get-tuple-element.7) | data formatting | bytes 25165824
